TPU v7x, 512 devices: a whole 4x4x16 slice. The times are simulated.
512 devices in a mesh: seq: 64 (over z, x), tp: 8 (over y, core).
Axes of the slice: x: 4, y: 4, z: 16, core: 2. Of those that a mesh axis runs over, the one named last changes fastest.
Arguments:
- x_in: bfloat16 [8192, 8192], P('seq', 'tp'), may hold values from -6 to 6
- bc_in: bfloat16 [8192, 2, 2048], P('seq', None, 'tp'), may hold values from -3 to 3
- z_in: bfloat16 [8192, 8192], P('seq', 'tp'), may hold values from -6 to 6
- dt_raw: bfloat16 [8192, 128], P('seq', 'tp'), may hold values from -5 to 5
- starts: int32 [8192], P('seq'), may hold values 0 or 1
- conv_x: float32 [4, 8192], P(None, 'tp'), may hold values from -3 to 3
- conv_bc: float32 [4, 2, 2048], P(None, None, 'tp'), may hold values from -3 to 3
- a_log: float32 [128], P('tp'), may hold values from -9 to -3
- dt_bias: float32 [128], P('tp'), may hold values from -2 to 1
- d_skip: float32 [128], P('tp'), may hold values from 0.5 to 2
- norm_gain: float32 [8192], P('tp'), may hold values from 0.5 to 1.5
Outputs:
- mixed: bfloat16 [8192, 8192], P('seq', 'tp')
All inputs are finite; a program needn't handle non-finite values. No bound on the sum of `starts` on one device may be relied on, other than what follows from the above.
Results may differ from a plain program's by a relative error of at most 0.0085.
Values may be sent and summed in bfloat16 or wider, within the bound.
A program may use at most 192 MiB of HBM per device.

v0:
```python
import jax
import jax.numpy as jnp
from jax import lax
from jax.sharding import PartitionSpec as P

BLOCK = 128


EPSILON = 1e-05


def from_behind(value, axis, steps):
    count = lax.axis_size(axis)
    first, last = (max(0, -steps), min(count, count - steps))
    return lax.ppermute(value, axis, [(source, source + steps) for source in range(first, last)])


def prefix(shard, axis, combine, identity):
    peers, mine = (lax.axis_size(axis), lax.axis_index(axis))
    everything = jax.tree.map(lambda part: lax.all_gather(part, axis), shard)
    start = jax.tree.map(
        lambda part, zero: jnp.broadcast_to(jnp.asarray(zero, part.dtype), part.shape),
        shard,
        identity,
    )

    def hop(k, before):
        reached = k < mine
        new = combine(before, jax.tree.map(lambda part: part[k], everything))
        return jax.tree.map(lambda a, b: jnp.where(reached, a, b), new, before)

    return lax.fori_loop(0, peers, hop, start)


def local_conv(values, tail_rows, taps, segment):
    count_rows = values.shape[0]
    reach = tail_rows.shape[0]
    padded = jnp.concatenate([tail_rows, values], 0)
    padded_segment = jnp.concatenate([jnp.zeros((reach,), jnp.int32), segment], 0)
    summed = jnp.zeros(values.shape, jnp.float32)
    for offset in range(reach + 1):
        shifted = lax.slice_in_dim(padded, reach - offset, reach - offset + count_rows, axis=0)
        shifted_segment = lax.slice_in_dim(
            padded_segment, reach - offset, reach - offset + count_rows, axis=0
        )
        valid_tap = (shifted_segment == segment).astype(jnp.float32)
        valid_tap = valid_tap.reshape((count_rows,) + (1,) * (values.ndim - 1))
        summed = summed + taps[reach - offset] * shifted.astype(jnp.float32) * valid_tap
    return jax.nn.silu(summed).astype(jnp.bfloat16)


def combine_states(earlier, later):
    return (earlier[0] * later[0], later[0][:, None, None] * earlier[1] + later[1])


def per_device(
    x_in, bc_in, z_in, dt_raw, starts, conv_x, conv_bc, a_log, dt_bias, d_skip, norm_gain
):
    length = x_in.shape[0]
    head_count = dt_raw.shape[1]
    head_dim = x_in.shape[1] // head_count
    state_dim = bc_in.shape[2]
    reach = conv_x.shape[0] - 1
    block_rows = BLOCK
    blocks = length // block_rows
    segment = jnp.cumsum(starts)
    tail_keep = (segment[length - reach :] == segment[length - 1]).astype(jnp.bfloat16)
    x_tail, bc_tail = from_behind(
        (
            x_in[length - reach :] * tail_keep[:, None],
            bc_in[length - reach :] * tail_keep[:, None, None],
        ),
        "seq",
        1,
    )
    x_conv = local_conv(x_in, x_tail, conv_x, segment)
    bc_conv = local_conv(bc_in, bc_tail, conv_bc, segment)
    x_blocks = x_conv.reshape(blocks, block_rows, head_count, head_dim)
    b_blocks = bc_conv[:, 0].reshape(blocks, block_rows, state_dim)
    c_blocks = bc_conv[:, 1].reshape(blocks, block_rows, state_dim)
    step_size = jax.nn.softplus(dt_raw.astype(jnp.float32) + dt_bias[None, :])
    log_decay = step_size * (-jnp.exp(a_log))[None, :]
    step_blocks = step_size.reshape(blocks, block_rows, head_count)
    cumulative = jnp.cumsum(log_decay.reshape(blocks, block_rows, head_count), axis=1)
    inner_seg = jnp.cumsum(starts.reshape(blocks, block_rows), axis=1)
    causal = jnp.arange(block_rows)[:, None] >= jnp.arange(block_rows)[None, :]
    linked = causal[None] & (inner_seg[:, :, None] == inner_seg[:, None, :])
    scores = jnp.einsum("kin,kjn->kij", c_blocks, b_blocks, preferred_element_type=jnp.float32)
    cum_heads = cumulative.transpose(0, 2, 1)
    log_gap = cum_heads[:, :, :, None] - cum_heads[:, :, None, :]
    mixing = jnp.where(linked[:, None], jnp.exp(jnp.minimum(log_gap, 0.0)), 0.0)
    mixing = mixing * scores[:, None] * step_blocks.transpose(0, 2, 1)[:, :, None, :]
    y_intra = jnp.einsum(
        "khij,kjhp->kihp", mixing.astype(jnp.bfloat16), x_blocks, preferred_element_type=jnp.float32
    )
    last_log = cumulative[:, -1]
    tail_linked = (inner_seg == inner_seg[:, -1:]).astype(jnp.float32)
    coefficient = jnp.exp(last_log[:, None] - cumulative) * step_blocks * tail_linked[:, :, None]
    weighted = (x_blocks * coefficient[..., None]).astype(jnp.bfloat16)
    block_states = jnp.einsum(
        "kjhp,kjn->khpn", weighted, b_blocks, preferred_element_type=jnp.float32
    )
    carried = jnp.exp(last_log) * (inner_seg[:, -1] == 0).astype(jnp.float32)[:, None]

    def advance(carry_pair, inputs):
        state_now, product = carry_pair
        decay_here, block_here = inputs
        return (
            (decay_here[:, None, None] * state_now + block_here, decay_here * product),
            (state_now, product),
        )

    empty_state = jnp.zeros((head_count, head_dim, state_dim), jnp.float32)
    unit_decay = jnp.ones((head_count,), jnp.float32)
    (end_state, end_decay), (start_states, start_decay) = lax.scan(
        advance, (empty_state, unit_decay), (carried, block_states)
    )
    enter_factor = jnp.exp(cumulative) * (inner_seg == 0).astype(jnp.float32)[:, :, None]
    c_float = c_blocks.astype(jnp.float32)
    incoming = prefix((end_decay, end_state), "seq", combine_states, (unit_decay, empty_state))[1]
    true_starts = start_states + start_decay[:, :, None, None] * incoming[None]
    y_state = enter_factor[..., None] * jnp.einsum(
        "kin,khpn->kihp", c_float, true_starts, precision=lax.Precision.HIGHEST
    )
    y_total = (y_intra + y_state).reshape(length, head_count, head_dim)
    y_total = y_total + d_skip[None, :, None] * x_conv.reshape(length, head_count, head_dim).astype(
        jnp.float32
    )
    gated_out = y_total * jax.nn.silu(
        z_in.reshape(length, head_count, head_dim).astype(jnp.float32)
    )
    square_total = lax.psum(jnp.sum(gated_out * gated_out, axis=(1, 2)), "tp")
    channels = head_count * head_dim * lax.axis_size("tp")
    inverse_rms = lax.rsqrt(square_total / channels + EPSILON)
    result = gated_out * inverse_rms[:, None, None] * norm_gain.reshape(head_count, head_dim)[None]
    return result.reshape(length, head_count * head_dim).astype(jnp.bfloat16)


def solution(mesh):
    return jax.shard_map(
        per_device,
        mesh=mesh,
        in_specs=(
            P("seq", "tp"),
            P("seq", None, "tp"),
            P("seq", "tp"),
            P("seq", "tp"),
            P("seq"),
            P(None, "tp"),
            P(None, None, "tp"),
            P("tp"),
            P("tp"),
            P("tp"),
            P("tp"),
        ),
        out_specs=P("seq", "tp"),
        check_vma=False,
    )
```

profile of v0, /device:TPU:480, one launch (start us, length us, event | category | flops | bytes accessed | tf_op | source)
XLA Modules:
  0.0 659.2 jit_solution(14677730130126385901)
XLA Ops:
  9.5 3.4 collective-permute-start
  13.9 3.4 collective-permute-start.1
  30.7 71.8 %all-gather = f32[64,1,16]{2,1,0:T(1,128)S(1)} all-gather(f32[1,1,16]{2,1,0:T(1,128)S(1)} %get-tuple-element.151), channel_id=2, replica_groups=mesh['seq'=64,'tp'=8] {'seq'}, dimensions={0}, use_global_device_ids=true | all-gather | bytes 4160 | tf_op jit(solution)/shard_map/all_gather | solution.py:20
  102.7 435.6 %all-gather.4.cloned.1.call-done = f32[1024,64,256]{2,1,0:T(8,128)} async-done(((f32[16,64,256]{2,1,0:T(8,128)}), f32[1024,64,256]{2,1,0:T(8,128)}) %all-gather.4.cloned.1.call-update) | async-done | bytes 67108880 | tf_op jit(solution)/shard_map/all_gather | solution.py:20
  538.2 96.1 %while.9 = (s32[]{:T(128)}, f32[16,64,256]{2,1,0:T(8,128)S(1)}, s32[]{:T(128)}, f32[64,16]{1,0:T(8,128)S(1)}, f32[64,16,64,256]{3,2,1,0:T(8,128)}, /*index=5*/s32[]{:T(128)}, s32[]{:T(128)}) while((s32[]{:T(128)}, f32[16,64,256]{2,1,0:T(8,128)S(1)}, s32[]{:T(128)}, f32[64,16]{1,0:T(8,128)S(1)}, f32[64,16,64,256]{3,2,1,0:T(8,128)}, ...), condition=%wide.region_4.5_spmd.clone, body=%wide.region_3.4_spmd.clone.sunk | while | flops 1048580 | bytes 3146025 | solution.py:32
  539.7 1.5 fusion.45
  541.2 1.5 fusion.45
  542.8 1.5 fusion.45
  544.3 1.5 fusion.45
  545.8 1.5 fusion.45
  547.3 1.5 fusion.45
  548.8 1.5 fusion.45
  550.3 1.5 fusion.45
  551.8 1.5 fusion.45
  557.8 1.5 fusion.45
  562.3 1.5 fusion.45
  563.8 1.5 fusion.45
  568.3 1.5 fusion.45
  574.3 1.5 fusion.45
  580.3 1.5 fusion.45
  586.3 1.5 fusion.45
  590.8 1.5 fusion.45
  592.3 1.5 fusion.45
  596.8 1.5 fusion.45
  602.8 1.5 fusion.45
  608.8 1.5 fusion.45
  614.9 1.5 fusion.45
  619.4 1.5 fusion.45
  620.9 1.5 fusion.45
  625.4 1.5 fusion.45
  631.4 1.5 fusion.45
  636.3 14.2 %psum.7 = f32[128]{0:T(128)S(1)} all-reduce(f32[128]{0:T(128)S(1)} %get-tuple-element.169), channel_id=1, replica_groups=mesh['seq'=64,'tp'=8] {'tp'}, use_global_device_ids=true, to_apply=%region_6.7 | all-reduce | flops 128 | bytes 1024 | tf_op jit(solution)/shard_map/psum | solution.py:132
  (145 shorter events, 76.7 us)
Async XLA Ops:
  6.5 531.7 %all-gather.4.cloned.1.call-start = ((), (), s32[]{:S(2)}) async-start(), calls=%async_computation | async-start | bytes 68157440 | tf_op jit(solution)/shard_map/all_gather | solution.py:20
  9.5 16.5 %collective-permute-start = (bf16[3,1024]{1,0:T(4,128)(2,1)S(1)}, bf16[3,1024]{1,0:T(4,128)(2,1)S(1)}, u32[]{:S(2)}, u32[]{:S(2)}) collective-permute-start(bf16[3,1024]{1,0:T(4,128)(2,1)S(1)} %slice_multiply_fusion), channel_id=1, source_target_pairs={{0,8},{8,16},{16,24},{24,32},{32,40},{40,48},{48,56},{56,64},{64,7... | collective-permute-start | bytes 18440 | tf_op jit(solution)/shard_map/ppermute | solution.py:15
  13.9 11.8 %collective-permute-start.1 = (bf16[3,2,256]{2,0,1:T(4,128)(2,1)S(1)}, bf16[3,2,256]{2,0,1:T(4,128)(2,1)S(1)}, u32[]{:S(2)}, u32[]{:S(2)}) collective-permute-start(bf16[3,2,256]{2,0,1:T(4,128)(2,1)S(1)} %slice_multiply_fusion.1), channel_id=1, source_target_pairs={{0,8},{8,16},{16,24},{24,32},{32,40},{40,48},{48,56},{56,64},{64,7... | collective-permute-start | bytes 9224 | tf_op jit(solution)/shard_map/ppermute | solution.py:15
Sparse Core Ops, SparseCore 0:
  28.8 509.4 all-gather.3
where the time goes:
time: 669 us; the launch traced here: 659 us
  waiting for transfers between devices  436 us (65%)
  other arithmetic  102 us (15%)
  blocking collectives  86 us (13%)
  between operations  14.2 us (2%)
  local copies, waits for them, and re-layouts  9.32 us (1%)
  starting transfers between devices  6.78 us (1%)
    all_gather x1, waiting for transfers between devices, prefix(): everything = jax.tree.map(lambda part: lax.all_gather(part, axis), shard)  436 us
    select_n x64, other arithmetic, hop(): return jax.tree.map(lambda a, b: jnp.where(reached, a, b), new, before)  93.5 us
    all_gather x1, blocking collectives, prefix(): everything = jax.tree.map(lambda part: lax.all_gather(part, axis), shard)  71.8 us
    psum x1, blocking collectives, per_device(): square_total = lax.psum(jnp.sum(gated_out * gated_out, axis=(1, 2)), 'tp')  14.2 us
  transfers between devices with their start and end apart: 3, of which 1 were waited for; matrix products, arithmetic and copies ran while one was open for 2% of the time, Pallas kernels for 0%

commit v1 on v0

v1 whole, which is shorter than its diff:
```python
import functools

import jax
import jax.numpy as jnp
from jax import lax
from jax.experimental import pallas as pl
from jax.experimental.pallas import tpu as pltpu
from jax.sharding import PartitionSpec as P

NX = 4
CHUNKS = 2
HALO = 16
REACH = 3
EPSILON = 1e-05
MESH = pl.DeviceIdType.MESH
F32, BF16 = jnp.float32, jnp.bfloat16


def dot(a, b):
    return jnp.dot(a, b, preferred_element_type=F32)


def dot_nt(a, b):
    return lax.dot_general(a, b, (((1,), (1,)), ((), ())), preferred_element_type=F32)


def dot_tn(a, b):
    return lax.dot_general(a, b, (((0,), (0,)), ((), ())), preferred_element_type=F32)


def iota(shape, axis):
    return lax.broadcasted_iota(jnp.int32, shape, axis)


def pieces(value, count):
    parts = []
    for _ in range(count):
        part = value.astype(BF16)
        parts.append(part)
        value = value - part.astype(F32)
    return jnp.concatenate(parts, axis=0)


def kernel(
    nz, nx, ntp,
    x_ref, bc_ref, z_ref, dt_ref, st_ref, cx_ref, cbc_ref, al_ref, db_ref, ds_ref, ng_ref,
    out_ref,
    xext, hsend, xc, crecv, dsend, drecv, tot_send, tot_recv,
    sbuf, srecv, lbuf, ylbuf, tbuf, zrecv, obuf, szbuf, ysend, yrecv,
    ebuf, yi, sz, gbuf, ssend, ssrecv,
    h_sem, d_sem, t_sem, c_sem, s_sem, zf_sem, zb_sem, y_sem, n_sem,
):
    seq, tp = lax.axis_index("seq"), lax.axis_index("tp")
    mz, mx = seq // nx, seq % nx
    nseq = nz * nx
    rows, channels = x_ref.shape
    state = bc_ref.shape[1] // 2
    heads = dt_ref.shape[0]
    quarter = channels // nx
    width = quarter // CHUNKS
    wide = HALO + rows

    def x_peer(r):
        q = (mx + r) % nx
        return q, {"seq": mz * nx + q}

    def z_peer(r):
        k = (mz + r) % nz
        return k, {"seq": k * nx + mx}

    def t_peer(r):
        return {"tp": (tp + r) % ntp}

    following, preceding = {"seq": (seq + 1) % nseq}, {"seq": (seq + nseq - 1) % nseq}

    def remote(src, dst, sem, device):
        return pltpu.make_async_remote_copy(
            src_ref=src, dst_ref=dst, send_sem=sem.at[0], recv_sem=sem.at[1],
            device_id=device, device_id_type=MESH,
        )

    barrier = pltpu.get_barrier_semaphore()

    def greet(device):
        pl.semaphore_signal(barrier, inc=1, device_id=device, device_id_type=MESH)

    greet(following)
    greet(preceding)
    for r in range(1, nx):
        greet(x_peer(r)[1])

    @pl.loop(1, nz)
    def _(r):
        greet(z_peer(r)[1])

    for r in range(1, ntp):
        greet(t_peer(r))

    starts = st_ref[...].astype(F32)
    starts_wide = jnp.broadcast_to(starts, (wide, rows)).astype(BF16)
    row, col = iota((rows, rows), 0), iota((rows, rows), 1)
    tril = (col <= row).astype(F32).astype(BF16)
    ranges = [tril, (col > row).astype(F32).astype(BF16)]
    for d in range(1, REACH + 1):
        ranges.append(((col <= row) & (col > row - d)).astype(F32).astype(BF16))
    counts = dot_nt(jnp.concatenate(ranges, axis=0), starts_wide)
    seg_col = counts[:rows, :rows]
    to_last = (counts[rows : 2 * rows, :rows] == 0.0).astype(F32)
    seg_row = dot_nt(starts_wide[:rows], tril)
    linked = (seg_col == seg_row) & (col <= row)
    from_first = (seg_col == 0.0).astype(F32)
    tap_row, tap_col = iota((rows, wide), 0), iota((rows, wide), 1)
    first_col = jnp.where(seq == 0, HALO, 0)
    taps = []
    for d in range(1, REACH + 1):
        none_between = counts[(d + 1) * rows : (d + 2) * rows] == 0.0
        place = (tap_col - HALO == tap_row - d) & (tap_col >= first_col)
        taps.append((place & none_between).astype(F32).astype(BF16))
    taps = jnp.concatenate(taps, axis=0)

    xext[HALO:, :channels] = x_ref[...]
    xext[HALO:, channels:] = bc_ref[...]
    keep = to_last[rows - HALO :, :1]
    hsend[...] = (xext[rows:, :].astype(F32) * keep).astype(BF16)

    raw = dt_ref[...].astype(F32) + db_ref[...]
    step = jnp.maximum(raw, 0.0) + jnp.log1p(jnp.exp(-jnp.abs(raw)))
    decay = -jnp.exp(al_ref[...]) * step
    parts = dot_nt(pieces(decay, 3), tril)
    cumulative = parts[:heads] + parts[heads : 2 * heads] + parts[2 * heads :]
    spread = (iota((heads, channels), 1) // (channels // heads) == iota((heads, channels), 0))
    spread = spread.astype(F32).astype(BF16)
    spread2 = jnp.concatenate([spread, spread], axis=0)
    ebuf[...] = dot_tn(pieces(jnp.exp(cumulative), 2), spread2)
    fall = ebuf[rows - 1 :, :]
    whole = (counts[rows - 1 : rows, :1] == 0.0).astype(F32)
    through = fall * whole
    for q in range(nx):
        for c in range(CHUNKS):
            at = q * quarter + c * width
            dsend[q, c : c + 1, :] = through[:, at : at + width]

    pl.semaphore_wait(barrier, (nx - 1) + (nz - 1) + (ntp - 1) + 2)

    halo = remote(hsend, xext.at[pl.ds(0, HALO)], h_sem, following)
    halo.start()
    for r in range(1, nx):
        q, device = x_peer(r)
        remote(dsend.at[q], drecv.at[mx], d_sem, device).start()
    drecv[mx] = dsend[mx]

    factor = dot_tn(pieces(jnp.exp(-cumulative) * step, 2), spread2)
    halo.wait_recv()

    def conv(at, size, weights):
        block = xext[:, at : at + size]
        shifted = dot(taps, block)
        total = weights[REACH] * block[HALO:].astype(F32)
        for d in range(1, REACH + 1):
            total += weights[REACH - d] * shifted[(d - 1) * rows : d * rows]
        return total * jax.nn.sigmoid(total)

    b = conv(channels, state, [cbc_ref[k, 0:1, :] for k in range(REACH + 1)])
    b = b.astype(BF16)
    bt = jnp.transpose(b.astype(F32) * to_last[:, :1]).astype(BF16)
    cc = conv(channels + state, state, [cbc_ref[k, 1:2, :] for k in range(REACH + 1)])
    cc = cc.astype(BF16)
    crecv[mx] = cc
    for r in range(1, nx):
        _, device = x_peer(r)
    fx = []
    for q in range(nx):
        at = q * quarter
        piece = conv(at, quarter, [cx_ref[k : k + 1, at : at + quarter] for k in range(REACH + 1)])
        piece = piece.astype(BF16)
        xc[:, at : at + quarter] = piece
        fx.append((piece.astype(F32) * factor[:, at : at + quarter]).astype(BF16))

    for c in range(CHUNKS):
        for q in range(nx):
            at = q * quarter + c * width
            made = dot(bt, fx[q][:, c * width : (c + 1) * width])
            sbuf[c, q] = (made * fall[:, at : at + width]).astype(BF16)
        for r in range(1, nx):
            q, device = x_peer(r)
            remote(sbuf.at[c, q], srecv.at[c, mx], s_sem.at[c], device).start()
        srecv[c, mx] = sbuf[c, mx]
    for r in range(1, nx):
        _, device = x_peer(r)
        remote(crecv.at[mx], crecv.at[mx], c_sem, device).start()

    def await_recv(buffer, count, sem):
        part = buffer.at[pl.ds(0, count)]
        remote(part, part, sem, following).wait_recv()

    def await_send(buffer, count, sem):
        part = buffer.at[pl.ds(0, count)]
        remote(part, part, sem, following).wait_send()

    await_recv(drecv, nx - 1, d_sem)
    reach_of = [None, drecv[0]]
    for k in range(1, nx):
        reach_of.append(reach_of[-1] * drecv[k])
    tot_send[...] = reach_of[nx]
    tot_recv[mz] = reach_of[nx]

    @pl.loop(1, nz)
    def _(r):
        k, device = z_peer(r)
        remote(tot_send, tot_recv.at[mz], t_sem, device).start()

    scores = jnp.where(linked, dot_nt(cc, b), 0.0).astype(BF16)
    for q in range(nx):
        at = q * quarter
        yi[:, at : at + quarter] = dot(scores, fx[q])
    gate = z_ref[...].astype(F32)
    sz[...] = gate * jax.nn.sigmoid(gate)

    for c in range(CHUNKS):
        await_recv(srecv.at[c], nx - 1, s_sem.at[c])
        running = srecv[c, 0].astype(F32)
        for k in range(1, nx):
            lbuf[c, k - 1] = running.astype(BF16)
            running = drecv[k, c : c + 1, :] * running + srecv[c, k].astype(F32)
        tbuf[c] = running.astype(BF16).reshape(nz, state // nz, width)
        zrecv[c, mz] = tbuf[c, mz]

        @pl.loop(1, nz)
        def _(r):
            k, device = z_peer(r)
            remote(tbuf.at[c, k], zrecv.at[c, mz], zf_sem.at[c], device).start()

    await_recv(crecv, nx - 1, c_sem)
    for c in range(CHUNKS):
        for k in range(1, nx):
            ylbuf[c, k - 1] = dot(crecv[k], lbuf[c, k - 1])

    await_recv(tot_recv, nz - 1, t_sem)
    for c in range(CHUNKS):
        await_recv(zrecv.at[c], nz - 1, zf_sem.at[c])
        running = jnp.zeros((state // nz, width), F32)
        for k in range(nz):
            obuf[c, k] = running.astype(BF16)
            running = tot_recv[k, c : c + 1, :] * running + zrecv[c, k].astype(F32)
        szbuf[c, mz] = obuf[c, mz]

        @pl.loop(1, nz)
        def _(r):
            k, device = z_peer(r)
            remote(obuf.at[c, k], szbuf.at[c, mz], zb_sem.at[c], device).start()

    for c in range(CHUNKS):
        await_recv(szbuf.at[c], nz - 1, zb_sem.at[c])
        entering = szbuf[c].reshape(state, width)
        for k in range(nx):
            part = dot(crecv[k], entering)
            if k:
                part = reach_of[k][c : c + 1, :] * part + ylbuf[c, k - 1]
            ysend[c, k] = part.astype(BF16)
        yrecv[c, mx] = ysend[c, mx]
        for r in range(1, nx):
            q, device = x_peer(r)
            remote(ysend.at[c, q], yrecv.at[c, mx], y_sem.at[c], device).start()

    skip = dot_tn(pieces(jnp.broadcast_to(ds_ref[...], (heads, 128)), 2), spread2)[:1]
    squares = jnp.zeros((rows, 128), F32)
    for c in range(CHUNKS):
        await_recv(yrecv.at[c], nx - 1, y_sem.at[c])
        for q in range(nx):
            at = slice(q * quarter + c * width, q * quarter + (c + 1) * width)
            y = yi[:, at] + from_first[:, :1] * yrecv[c, q].astype(F32)
            y = ebuf[:, at] * y + skip[:, at] * xc[:, at].astype(F32)
            gated = y * sz[:, at]
            gbuf[:, at] = gated
            for k in range(0, width, 128):
                part = gated[:, k : k + 128]
                squares += part * part
    total = jnp.sum(jnp.transpose(squares), axis=0, keepdims=True)
    total = jnp.broadcast_to(total, ssend.shape)
    ssend[...] = total
    ssrecv[tp] = total
    for r in range(1, ntp):
        remote(ssend, ssrecv.at[tp], n_sem, t_peer(r)).start()
    await_recv(ssrecv, ntp - 1, n_sem)
    total = jnp.sum(ssrecv[...], axis=0)[:1]
    inverse = lax.rsqrt(total / (channels * ntp) + EPSILON)
    inverse = jnp.transpose(jnp.broadcast_to(inverse, (rows, rows)))
    for at in range(0, channels, 128):
        at = slice(at, at + 128)
        out_ref[:, at] = (gbuf[:, at] * inverse * ng_ref[:, at]).astype(BF16)

    halo.wait_send()
    await_send(drecv, nx - 1, d_sem)
    await_send(tot_recv, nz - 1, t_sem)
    await_send(crecv, nx - 1, c_sem)
    for c in range(CHUNKS):
        await_send(srecv.at[c], nx - 1, s_sem.at[c])
        await_send(zrecv.at[c], nz - 1, zf_sem.at[c])
        await_send(szbuf.at[c], nz - 1, zb_sem.at[c])
        await_send(yrecv.at[c], nx - 1, y_sem.at[c])
    await_send(ssrecv, ntp - 1, n_sem)


def per_device(
    x_in, bc_in, z_in, dt_raw, starts, conv_x, conv_bc, a_log, dt_bias, d_skip, norm_gain
):
    rows, channels = x_in.shape
    state = bc_in.shape[2]
    heads = dt_raw.shape[1]
    nx, ntp = NX, lax.axis_size("tp")
    nz = lax.axis_size("seq") // nx
    width = channels // nx // CHUNKS
    vmem = pl.BlockSpec(memory_space=pltpu.VMEM)
    sems = pltpu.SemaphoreType.DMA
    return pl.pallas_call(
        functools.partial(kernel, nz, nx, ntp),
        out_shape=jax.ShapeDtypeStruct((rows, channels), BF16),
        in_specs=[vmem] * 11,
        out_specs=vmem,
        scratch_shapes=[
            pltpu.VMEM((HALO + rows, channels + 2 * state), BF16),
            pltpu.VMEM((HALO, channels + 2 * state), BF16),
            pltpu.VMEM((rows, channels), BF16),
            pltpu.VMEM((nx, rows, state), BF16),
            pltpu.VMEM((nx, CHUNKS, width), F32),
            pltpu.VMEM((nx, CHUNKS, width), F32),
            pltpu.VMEM((CHUNKS, width), F32),
            pltpu.VMEM((nz, CHUNKS, width), F32),
            pltpu.VMEM((CHUNKS, nx, state, width), BF16),
            pltpu.VMEM((CHUNKS, nx, state, width), BF16),
            pltpu.VMEM((CHUNKS, nx - 1, state, width), BF16),
            pltpu.VMEM((CHUNKS, nx - 1, rows, width), F32),
            pltpu.VMEM((CHUNKS, nz, state // nz, width), BF16),
            pltpu.VMEM((CHUNKS, nz, state // nz, width), BF16),
            pltpu.VMEM((CHUNKS, nz, state // nz, width), BF16),
            pltpu.VMEM((CHUNKS, nz, state // nz, width), BF16),
            pltpu.VMEM((CHUNKS, nx, rows, width), BF16),
            pltpu.VMEM((CHUNKS, nx, rows, width), BF16),
            pltpu.VMEM((rows, channels), F32),
            pltpu.VMEM((rows, channels), F32),
            pltpu.VMEM((rows, channels), F32),
            pltpu.VMEM((rows, channels), F32),
            pltpu.VMEM((8, 128), F32),
            pltpu.VMEM((ntp, 8, 128), F32),
            sems((2,)),
            sems((2,)),
            sems((2,)),
            sems((2,)),
            sems((CHUNKS, 2)),
            sems((CHUNKS, 2)),
            sems((CHUNKS, 2)),
            sems((CHUNKS, 2)),
            sems((2,)),
        ],
        compiler_params=pltpu.CompilerParams(
            collective_id=0, has_side_effects=True, vmem_limit_bytes=32 * 2**20
        ),
        cost_estimate=pl.CostEstimate(flops=2 * 10**8, bytes_accessed=2**20, transcendentals=10**6),
    )(
        x_in,
        bc_in.reshape(rows, 2 * state),
        z_in,
        dt_raw.T,
        starts.reshape(1, rows),
        conv_x,
        conv_bc,
        a_log.reshape(heads, 1),
        dt_bias.reshape(heads, 1),
        d_skip.reshape(heads, 1),
        norm_gain.reshape(1, channels),
    )


def solution(mesh):
    return jax.shard_map(
        per_device,
        mesh=mesh,
        in_specs=(
            P("seq", "tp"),
            P("seq", None, "tp"),
            P("seq", "tp"),
            P("seq", "tp"),
            P("seq"),
            P(None, "tp"),
            P(None, None, "tp"),
            P("tp"),
            P("tp"),
            P("tp"),
            P("tp"),
        ),
        out_specs=P("seq", "tp"),
        check_vma=False,
    )
```

time: 669 us -> 62.4 us (0.09)
  the two profiles are of different devices: /device:TPU:480 before, /device:TPU:1 now
where the time goes in v1:
time: 62.4 us; the launch traced here: 62.2 us
  Pallas kernels  56.6 us (91%)
  local copies, waits for them, and re-layouts  5.48 us (9%)
    pallas_call x1, Pallas kernels, per_device(): pl.pallas_call(functools.partial(kernel, nz, nx, ntp), out_shape=jax.Shap...  56.6 us
    unnamed x16, local copies, waits for them, and re-layouts  3.24 us

profile of v1, /device:TPU:1, one launch (start us, length us, event | category | flops | bytes accessed | tf_op | source)
XLA Modules:
  0.0 62.2 jit_solution(7167727355461822222)
XLA Ops:
  0.0 0.0 copy-start
  0.0 0.8 %copy.12.al_ref = f32[16,1]{1,0:T(8,128)S(1)} copy(f32[16,1]{0,1:T(1,128)} %bitcast.13) | data formatting | bytes 128 | tf_op jit(solution)/shard_map/reshape | solution.py:367
  0.8 0.7 %copy.13.db_ref = f32[16,1]{1,0:T(8,128)S(1)} copy(f32[16,1]{0,1:T(1,128)} %bitcast.14) | data formatting | bytes 128 | tf_op jit(solution)/shard_map/reshape | solution.py:368
  1.5 0.7 %copy.14.ds_ref = f32[16,1]{1,0:T(8,128)S(1)} copy(f32[16,1]{0,1:T(1,128)} %bitcast.15) | data formatting | bytes 128 | tf_op jit(solution)/shard_map/reshape | solution.py:369
  2.2 0.0 copy-start.2
  2.2 0.0 copy-start.3
  2.2 0.0 copy-start.4
  2.2 0.0 copy-start.5
  2.3 1.0 %copy.15 = bf16[16,8,2,256]{3,1,2,0:T(8,128)(2,1)S(1)} copy(bf16[16,8,2,256]{3,2,1,0:T(2,128)(2,1)} %bitcast.12) | data formatting | bytes 262144
  3.2 0.0 copy-start.6
  3.2 0.0 copy-done
  3.2 0.0 copy-done.2
  3.3 0.0 copy-done.3
  3.3 0.0 copy-done.4
  3.3 0.0 copy-done.5
  3.3 0.6 copy-done.6
  3.9 0.0 copy-start.1
  3.9 0.9 %copy-done.1 = bf16[128,1024]{1,0:T(8,128)(2,1)S(1)} copy-done((bf16[128,1024]{1,0:T(8,128)(2,1)S(1)}, bf16[128,1024]{1,0:T(8,128)(2,1)}, u32[]{:S(2)}) %copy-start.1) | copy-done | bytes 262168
  4.8 56.6 %shard_map.109 = bf16[128,1024]{1,0:T(8,128)(2,1)S(1)} custom-call(bf16[128,1024]{1,0:T(8,128)(2,1)S(1)} %copy-done, bf16[128,512]{1,0:T(8,128)(2,1)S(1)} %bitcast.8, bf16[128,1024]{1,0:T(8,128)(2,1)S(1)} %copy-done.1, bf16[16,128]{1,0:T(8,128)(2,1)S(1)} %bitcast.9, s32[1,128]{1,0:T(1,128)S(1)} %bitcast.11, f32[4,1024]{1,0:T(4,128)S(1)} %copy-done.2, ...), custom_call_target="tpu_custom_call" | custom-call | flops 200000000 | bytes 1048576 | tf_op jit(solution)/shard_map/pallas_call | solution.py:315
  61.5 0.7 %copy.17 = bf16[128,1024]{1,0:T(8,128)(2,1)} copy(bf16[128,1024]{1,0:T(8,128)(2,1)S(1)} %shard_map.109) | data formatting | bytes 524288
Async XLA Ops:
  0.0 3.2 %copy-start = (bf16[128,1024]{1,0:T(8,128)(2,1)S(1)}, bf16[128,1024]{1,0:T(8,128)(2,1)}, u32[]{:S(2)}) copy-start(bf16[128,1024]{1,0:T(8,128)(2,1)} %x_ref.1) | copy-start | bytes 786436
  2.2 1.0 %copy-start.2 = (f32[4,1024]{1,0:T(4,128)S(1)}, f32[4,1024]{1,0:T(4,128)}, u32[]{:S(2)}) copy-start(f32[4,1024]{1,0:T(4,128)} %cx_ref.1) | copy-start | bytes 49156
  2.2 1.0 %copy-start.3 = (f32[4,2,256]{2,1,0:T(2,128)S(1)}, f32[4,2,256]{2,1,0:T(2,128)}, u32[]{:S(2)}) copy-start(f32[4,2,256]{2,1,0:T(2,128)} %cbc_ref.1) | copy-start | bytes 24580
  2.2 1.0 %copy-start.4 = (bf16[128,16]{0,1:T(8,128)(2,1)S(1)}, bf16[128,16]{0,1:T(8,128)(2,1)}, u32[]{:S(2)}) copy-start(bf16[128,16]{0,1:T(8,128)(2,1)} %param.14) | copy-start | bytes 12292
  2.2 1.0 %copy-start.5 = (f32[1024]{0:T(1024)S(1)}, f32[1024]{0:T(1024)}, u32[]{:S(2)}) copy-start(f32[1024]{0:T(1024)} %param.21) | copy-start | bytes 12292
  3.2 0.7 %copy-start.6 = (s32[128]{0:T(128)S(1)}, s32[128]{0:T(128)}, u32[]{:S(2)}) copy-start(s32[128]{0:T(128)} %param.15) | copy-start | bytes 1540
  3.9 0.9 %copy-start.1 = (bf16[128,1024]{1,0:T(8,128)(2,1)S(1)}, bf16[128,1024]{1,0:T(8,128)(2,1)}, u32[]{:S(2)}) copy-start(bf16[128,1024]{1,0:T(8,128)(2,1)} %z_ref.1) | copy-start | bytes 786436

commit v2 on v1

v2 whole, which is shorter than its diff:
```python
import functools

import jax
import jax.numpy as jnp
from jax import lax
from jax.experimental import pallas as pl
from jax.experimental.pallas import tpu as pltpu
from jax.sharding import PartitionSpec as P

NX = 4
GROUP = 4
CHUNKS = 2
HEAD = 16
REACH = 3
FOLD = 4
EPSILON = 1e-05
MESH = pl.DeviceIdType.MESH
F32, BF16 = jnp.float32, jnp.bfloat16


def dot(a, b):
    return jnp.dot(a, b, preferred_element_type=F32)


def dot_nt(a, b):
    return lax.dot_general(a, b, (((1,), (1,)), ((), ())), preferred_element_type=F32)


def dot_tn(a, b):
    return lax.dot_general(a, b, (((0,), (0,)), ((), ())), preferred_element_type=F32)


def iota(shape, axis):
    return lax.broadcasted_iota(jnp.int32, shape, axis)


def pieces(value, count):
    parts = []
    for _ in range(count):
        part = value.astype(BF16)
        parts.append(part)
        value = value - part.astype(F32)
    return jnp.concatenate(parts, axis=0)


def silu(value):
    return value * jax.nn.sigmoid(value)


def kernel(
    nz, nx, ntp,
    x_hbm, bc_hbm, z_hbm, dt_hbm, st_hbm, cx_hbm, cbc_hbm, al_hbm, db_hbm, ds_hbm, ng_hbm,
    out_ref,
    x_ref, bc_ref, z_ref, dt_ref, st_ref, cx_ref, cbc_ref, al_ref, db_ref, ds_ref, ng_ref,
    hsend, hrecv, pre, weights, xc, fx, bcv, crecv, dsend, drecv, tot_send, tot_recv,
    sbuf, srecv, lbuf, ylbuf, tbuf, zrecv, prebuf, pout, pin, obuf, szbuf, ysend, yrecv,
    ebuf, yi, sz, gbuf, ssend, ssrecv,
    in_sem, h_sem, d_sem, t_sem, c_sem, s_sem, zf_sem, p_sem, zb_sem, y_sem, n_sem, near_sem,
):
    seq, tp = lax.axis_index("seq"), lax.axis_index("tp")
    mz, mx = seq // nx, seq % nx
    nseq, ngroups = nz * nx, nz // GROUP
    group, member = mz // GROUP, mz % GROUP
    rows, channels = x_ref.shape
    state = bc_ref.shape[2]
    heads = dt_ref.shape[0]
    quarter = channels // nx
    width = quarter // CHUNKS
    total_width = channels + 2 * state
    part = state // GROUP

    def seq_at(z, x):
        return {"seq": z * nx + x}

    def x_peer(r):
        q = (mx + r) % nx
        return q, seq_at(mz, q)

    def z_peer(r):
        k = (member + r) % GROUP
        return k, seq_at(group * GROUP + k, mx)

    def t_peer(r):
        return {"tp": (tp + r) % ntp}

    following, preceding = {"seq": seq + 1}, {"seq": seq - 1}
    next_group = seq_at(mz + GROUP, mx)

    def remote(src, dst, sem, device):
        return pltpu.make_async_remote_copy(
            src_ref=src, dst_ref=dst, send_sem=sem.at[0], recv_sem=sem.at[1],
            device_id=device, device_id_type=MESH,
        )

    def await_recv(buffer, count, sem):
        some = buffer.at[pl.ds(0, count)]
        remote(some, some, sem, x_peer(1)[1]).wait_recv()

    def await_send(buffer, count, sem):
        some = buffer.at[pl.ds(0, count)]
        remote(some, some, sem, x_peer(1)[1]).wait_send()

    loads = [
        pltpu.make_async_copy(src, dst, in_sem.at[k])
        for k, (src, dst) in enumerate([
            (st_hbm, st_ref), (dt_hbm, dt_ref), (al_hbm, al_ref), (db_hbm, db_ref),
            (x_hbm, x_ref), (bc_hbm, bc_ref), (cx_hbm, cx_ref), (cbc_hbm, cbc_ref),
            (z_hbm, z_ref), (ds_hbm, ds_ref), (ng_hbm, ng_ref),
        ])
    ]
    for load in loads:
        load.start()

    barrier = pltpu.get_barrier_semaphore()

    def greet(device, sem=barrier):
        pl.semaphore_signal(sem, inc=1, device_id=device, device_id_type=MESH)

    def greet_along_z(distance, sem):
        @pl.when(mz >= distance)
        def _():
            greet(seq_at(mz - distance, mx), sem)

        @pl.when(mz + distance < nz)
        def _():
            greet(seq_at(mz + distance, mx), sem)

    def both(distance):
        return (mz >= distance).astype(jnp.int32) + (mz + distance < nz).astype(jnp.int32)

    for r in range(1, nx):
        greet(x_peer(r)[1])
    for r in range(2, GROUP):
        @pl.when(member >= r)
        def _():
            greet(seq_at(mz - r, mx))

        @pl.when(member + r < GROUP)
        def _():
            greet(seq_at(mz + r, mx))

    greet_along_z(1, barrier)

    @pl.when(seq > 0)
    def _():
        greet(preceding)

    for r in range(1, ntp):
        greet(t_peer(r))
    greeted = (nx - 1) + (ntp - 1) + both(1) + (seq + 1 < nseq).astype(jnp.int32)
    for r in range(2, GROUP):
        greeted += (member >= r).astype(jnp.int32) + (member + r < GROUP).astype(jnp.int32)

    row, col = iota((rows, rows), 0), iota((rows, rows), 1)
    tril = (col <= row).astype(F32).astype(BF16)
    ranges = [tril, (col > row).astype(F32).astype(BF16)]
    for d in range(1, REACH + 1):
        ranges.append(((col <= row) & (col > row - d)).astype(F32).astype(BF16))
    spread = iota((heads, channels), 1) // (channels // heads) == iota((heads, channels), 0)
    spread = spread.astype(F32).astype(BF16)
    spread2 = jnp.concatenate([spread, spread], axis=0)
    for load in loads[:4]:
        load.wait()
    starts = jnp.broadcast_to(st_ref[...].astype(F32), (rows, rows)).astype(BF16)
    counts = dot_nt(jnp.concatenate(ranges, axis=0), starts)
    seg_col = counts[:rows]
    to_last = (counts[rows : 2 * rows] == 0.0).astype(F32)
    linked = (seg_col == dot_nt(starts, tril)) & (col <= row)
    from_first = (seg_col == 0.0).astype(F32)
    none_between = [counts[(d + 1) * rows : (d + 2) * rows] == 0.0 for d in range(1, REACH + 1)]
    taps = jnp.concatenate(
        [((col == row - d) & none_between[d - 1]).astype(F32).astype(BF16) for d in range(1, REACH + 1)],
        axis=0,
    )

    for load in loads[4:8]:
        load.wait()
    weights[:, :channels] = cx_ref[...]
    for k in range(REACH + 1):
        weights[k : k + 1, channels : channels + state] = cbc_ref[k, 0:1, :]
        weights[k : k + 1, channels + state :] = cbc_ref[k, 1:2, :]
    b_in, c_in = bc_ref[:, 0, :], bc_ref[:, 1, :]

    tail = slice(rows - 8, rows)
    last_rows = jnp.concatenate(
        [x_ref[tail, :].astype(F32), b_in[tail].astype(F32), c_in[tail].astype(F32)], axis=1
    )
    last_rows = (last_rows * to_last[tail, :1])[8 - FOLD :]
    piece = total_width // FOLD
    hsend[...] = jnp.concatenate(
        [last_rows[:, k * piece : (k + 1) * piece] for k in range(FOLD)], axis=0
    ).astype(BF16)

    def column(ref):
        square = (heads, heads)
        here = iota(square, 0) == iota(square, 1)
        return jnp.sum(jnp.where(here, jnp.broadcast_to(ref[...], square), 0.0), axis=1, keepdims=True)

    raw = dt_ref[...].astype(F32) + column(db_ref)
    step = jnp.maximum(raw, 0.0) + jnp.log1p(jnp.exp(-jnp.abs(raw)))
    decay = -jnp.exp(column(al_ref)) * step
    parts = dot_nt(pieces(decay, 3), tril)
    cumulative = parts[:heads] + parts[heads : 2 * heads] + parts[2 * heads :]
    ebuf[...] = dot_tn(pieces(jnp.exp(cumulative), 2), spread2)
    fall = ebuf[rows - 1 :, :]
    through = fall * (seg_col[rows - 1 : rows, :1] == 0.0).astype(F32)
    for q in range(nx):
        for c in range(CHUNKS):
            at = q * quarter + c * width
            dsend[q, c : c + 1, :] = through[:, at : at + width]
    factor = dot_tn(pieces(jnp.exp(-cumulative) * step, 2), spread2)

    def conv(values, at):
        size = values.shape[1]
        taken = weights[:, at : at + size]
        shifted = dot(taps, values)
        total = taken[REACH:] * values.astype(F32)
        for d in range(1, REACH + 1):
            total += taken[REACH - d : REACH - d + 1] * shifted[(d - 1) * rows : d * rows]
        pre[:, at : at + size] = total[:HEAD]
        return silu(total)

    bcv[:, :state] = conv(b_in, channels).astype(BF16)
    bcv[:, state:] = conv(c_in, channels + state).astype(BF16)
    for at in range(0, channels, 256):
        xc[:, at : at + 256] = conv(x_ref[:, at : at + 256], at).astype(BF16)

    pl.semaphore_wait(barrier, greeted)

    halo = remote(hsend, hrecv, h_sem, following)

    @pl.when(seq + 1 < nseq)
    def _():
        halo.start()

    greet_along_z(1, near_sem.at[0])
    for r in range(1, nx):
        q, device = x_peer(r)
        remote(dsend.at[q], drecv.at[mx], d_sem, device).start()
    drecv[mx] = dsend[mx]
    for at in range(0, channels, 256):
        at = slice(at, at + 256)
        fx[HEAD:, at] = (xc[HEAD:, at].astype(F32) * factor[HEAD:, at]).astype(BF16)

    @pl.when(seq == 0)
    def _():
        hrecv[...] = jnp.zeros(hrecv.shape, BF16)

    @pl.when(seq > 0)
    def _():
        halo.wait_recv()

    place_row, place_col = iota((HEAD, HEAD), 0), iota((HEAD, HEAD), 1)
    for k in range(FOLD):
        at = slice(k * piece, (k + 1) * piece)
        reached = []
        for d in range(1, REACH + 1):
            here = (place_col - (k + 1) * FOLD == place_row - d) & (place_row < d)
            here &= none_between[d - 1][:HEAD, :HEAD] & (place_col >= k * FOLD)
            reached.append(here.astype(F32).astype(BF16))
        added = dot(jnp.concatenate(reached, axis=0), hrecv[...])
        total = pre[:, at]
        for d in range(1, REACH + 1):
            total += weights[REACH - d : REACH - d + 1, at] * added[(d - 1) * HEAD : d * HEAD]
        pre[:, at] = total
    done = silu(pre[...]).astype(BF16)
    xc[:HEAD, :] = done[:, :channels]
    bcv[:HEAD, :] = done[:, channels:]
    fx[:HEAD, :] = (done[:, :channels].astype(F32) * factor[:HEAD]).astype(BF16)
    b = bcv[:, :state]
    bt = jnp.transpose(b.astype(F32) * to_last[:, :1]).astype(BF16)

    for c in range(CHUNKS):
        for q in range(nx):
            at = slice(q * quarter + c * width, q * quarter + (c + 1) * width)
            sbuf[c, q] = (dot(bt, fx[:, at]) * fall[:, at]).astype(BF16)
        for r in range(1, nx):
            q, device = x_peer(r)
            remote(sbuf.at[c, q], srecv.at[c, mx], s_sem.at[c], device).start()
        srecv[c, mx] = sbuf[c, mx]
    cc = bcv[:, state:]
    crecv[mx] = cc
    for r in range(1, nx):
        _, device = x_peer(r)
        remote(crecv.at[mx], crecv.at[mx], c_sem, device).start()

    await_recv(drecv, nx - 1, d_sem)
    reach_of = [None, drecv[0]]
    for k in range(1, nx):
        reach_of.append(reach_of[-1] * drecv[k])
    tot_send[...] = reach_of[nx]
    tot_recv[member] = reach_of[nx]
    for r in range(1, GROUP):
        k, device = z_peer(r)
        remote(tot_send, tot_recv.at[member], t_sem, device).start()
    pl.semaphore_wait(near_sem.at[0], both(1))
    if GROUP > 2:
        greet_along_z(2, near_sem.at[1])

    scores = jnp.where(linked, dot_nt(cc, b), 0.0).astype(BF16)
    for q in range(nx):
        at = slice(q * quarter, (q + 1) * quarter)
        yi[:, at] = dot(scores, fx[:, at])
    for load in loads[8:]:
        load.wait()
    sz[...] = silu(z_ref[...].astype(F32))

    for c in range(CHUNKS):
        await_recv(srecv.at[c], nx - 1, s_sem.at[c])
        running = srecv[c, 0].astype(F32)
        for k in range(1, nx):
            lbuf[c, k - 1] = running.astype(BF16)
            running = drecv[k, c : c + 1, :] * running + srecv[c, k].astype(F32)
        tbuf[c] = running.astype(BF16).reshape(GROUP, part, width)
        zrecv[c, member] = tbuf[c, member]
        for r in range(1, GROUP):
            k, device = z_peer(r)
            remote(tbuf.at[c, k], zrecv.at[c, member], zf_sem.at[c], device).start()

    await_recv(crecv, nx - 1, c_sem)
    for c in range(CHUNKS):
        for k in range(1, nx):
            ylbuf[c, k - 1] = dot(crecv[k], lbuf[c, k - 1])

    if GROUP > 2:
        pl.semaphore_wait(near_sem.at[1], both(2))
    await_recv(tot_recv, GROUP - 1, t_sem)
    row_fall = [tot_recv[k] for k in range(GROUP)]
    for c in range(CHUNKS):
        await_recv(zrecv.at[c], GROUP - 1, zf_sem.at[c])
        running = zrecv[c, 0].astype(F32)
        reach = row_fall[0][c : c + 1]
        for k in range(1, GROUP):
            prebuf[c, k] = running
            running = row_fall[k][c : c + 1] * running + zrecv[c, k].astype(F32)
            reach = row_fall[k][c : c + 1] * reach

        @pl.when(group == 0)
        def _():
            pin[c] = jnp.zeros(pin.shape[1:], BF16)

        @pl.when(group > 0)
        def _():
            remote(pout.at[c], pin.at[c], p_sem.at[c], next_group).wait_recv()

        before = pin[c].astype(F32)

        @pl.when(group + 1 < ngroups)
        def _():
            pout[c] = (reach * before + running).astype(BF16)
            remote(pout.at[c], pin.at[c], p_sem.at[c], next_group).start()

        obuf[c, 0] = pin[c]
        reach = row_fall[0][c : c + 1]
        for k in range(1, GROUP):
            obuf[c, k] = (reach * before + prebuf[c, k]).astype(BF16)
            reach = row_fall[k][c : c + 1] * reach
        szbuf[c, member] = obuf[c, member]
        for r in range(1, GROUP):
            k, device = z_peer(r)
            remote(obuf.at[c, k], szbuf.at[c, member], zb_sem.at[c], device).start()

    for c in range(CHUNKS):
        await_recv(szbuf.at[c], GROUP - 1, zb_sem.at[c])
        entering = szbuf[c].reshape(state, width)
        for k in range(nx):
            part_y = dot(crecv[k], entering)
            if k:
                part_y = reach_of[k][c : c + 1, :] * part_y + ylbuf[c, k - 1]
            ysend[c, k] = part_y.astype(BF16)
        yrecv[c, mx] = ysend[c, mx]
        for r in range(1, nx):
            q, device = x_peer(r)
            remote(ysend.at[c, q], yrecv.at[c, mx], y_sem.at[c], device).start()

    skip = dot_tn(pieces(jnp.broadcast_to(column(ds_ref), (heads, 128)), 2), spread2)[:1]
    squares = jnp.zeros((rows, 128), F32)
    for c in range(CHUNKS):
        await_recv(yrecv.at[c], nx - 1, y_sem.at[c])
        for q in range(nx):
            at = slice(q * quarter + c * width, q * quarter + (c + 1) * width)
            y = yi[:, at] + from_first[:, :1] * yrecv[c, q].astype(F32)
            y = ebuf[:, at] * y + skip[:, at] * xc[:, at].astype(F32)
            gated = y * sz[:, at]
            gbuf[:, at] = gated
            for k in range(0, width, 128):
                some = gated[:, k : k + 128]
                squares += some * some
    total = jnp.sum(jnp.transpose(squares), axis=0, keepdims=True)
    total = jnp.broadcast_to(total, ssend.shape)
    ssend[...] = total
    ssrecv[tp] = total
    for r in range(1, ntp):
        remote(ssend, ssrecv.at[tp], n_sem, t_peer(r)).start()
    await_recv(ssrecv, ntp - 1, n_sem)
    total = jnp.sum(ssrecv[...], axis=0)[:1]
    inverse = lax.rsqrt(total / (channels * ntp) + EPSILON)
    inverse = jnp.transpose(jnp.broadcast_to(inverse, (rows, rows)))
    for at in range(0, channels, 128):
        at = slice(at, at + 128)
        out_ref[:, at] = (gbuf[:, at] * inverse * ng_ref[:, at]).astype(BF16)

    @pl.when(seq + 1 < nseq)
    def _():
        halo.wait_send()

    await_send(drecv, nx - 1, d_sem)
    await_send(tot_recv, GROUP - 1, t_sem)
    await_send(crecv, nx - 1, c_sem)
    for c in range(CHUNKS):
        await_send(srecv.at[c], nx - 1, s_sem.at[c])
        await_send(zrecv.at[c], GROUP - 1, zf_sem.at[c])

        @pl.when(group + 1 < ngroups)
        def _():
            remote(pout.at[c], pin.at[c], p_sem.at[c], next_group).wait_send()

        await_send(szbuf.at[c], GROUP - 1, zb_sem.at[c])
        await_send(yrecv.at[c], nx - 1, y_sem.at[c])
    await_send(ssrecv, ntp - 1, n_sem)


def per_device(
    x_in, bc_in, z_in, dt_raw, starts, conv_x, conv_bc, a_log, dt_bias, d_skip, norm_gain
):
    rows, channels = x_in.shape
    state = bc_in.shape[2]
    heads = dt_raw.shape[1]
    nx, ntp = NX, lax.axis_size("tp")
    nz = lax.axis_size("seq") // nx
    width = channels // nx // CHUNKS
    total_width = channels + 2 * state
    part = state // GROUP
    operands = (
        x_in,
        bc_in,
        z_in,
        dt_raw.T,
        starts.reshape(1, rows),
        conv_x,
        conv_bc,
        a_log.reshape(1, heads),
        dt_bias.reshape(1, heads),
        d_skip.reshape(1, heads),
        norm_gain.reshape(1, channels),
    )
    sems = pltpu.SemaphoreType.DMA
    return pl.pallas_call(
        functools.partial(kernel, nz, nx, ntp),
        out_shape=jax.ShapeDtypeStruct((rows, channels), BF16),
        in_specs=[pl.BlockSpec(memory_space=pltpu.HBM)] * len(operands),
        out_specs=pl.BlockSpec(memory_space=pltpu.VMEM),
        scratch_shapes=[
            *(pltpu.VMEM(operand.shape, operand.dtype) for operand in operands),
            pltpu.VMEM((4 * FOLD, total_width // FOLD), BF16),
            pltpu.VMEM((4 * FOLD, total_width // FOLD), BF16),
            pltpu.VMEM((HEAD, total_width), F32),
            pltpu.VMEM((REACH + 1, total_width), F32),
            pltpu.VMEM((rows, channels), BF16),
            pltpu.VMEM((rows, channels), BF16),
            pltpu.VMEM((rows, 2 * state), BF16),
            pltpu.VMEM((nx, rows, state), BF16),
            pltpu.VMEM((nx, CHUNKS, width), F32),
            pltpu.VMEM((nx, CHUNKS, width), F32),
            pltpu.VMEM((CHUNKS, width), F32),
            pltpu.VMEM((GROUP, CHUNKS, width), F32),
            pltpu.VMEM((CHUNKS, nx, state, width), BF16),
            pltpu.VMEM((CHUNKS, nx, state, width), BF16),
            pltpu.VMEM((CHUNKS, nx - 1, state, width), BF16),
            pltpu.VMEM((CHUNKS, nx - 1, rows, width), F32),
            pltpu.VMEM((CHUNKS, GROUP, part, width), BF16),
            pltpu.VMEM((CHUNKS, GROUP, part, width), BF16),
            pltpu.VMEM((CHUNKS, GROUP, part, width), F32),
            pltpu.VMEM((CHUNKS, part, width), BF16),
            pltpu.VMEM((CHUNKS, part, width), BF16),
            pltpu.VMEM((CHUNKS, GROUP, part, width), BF16),
            pltpu.VMEM((CHUNKS, GROUP, part, width), BF16),
            pltpu.VMEM((CHUNKS, nx, rows, width), BF16),
            pltpu.VMEM((CHUNKS, nx, rows, width), BF16),
            pltpu.VMEM((rows, channels), F32),
            pltpu.VMEM((rows, channels), F32),
            pltpu.VMEM((rows, channels), F32),
            pltpu.VMEM((rows, channels), F32),
            pltpu.VMEM((8, 128), F32),
            pltpu.VMEM((ntp, 8, 128), F32),
            sems((len(operands),)),
            sems((2,)),
            sems((2,)),
            sems((2,)),
            sems((2,)),
            sems((CHUNKS, 2)),
            sems((CHUNKS, 2)),
            sems((CHUNKS, 2)),
            sems((CHUNKS, 2)),
            sems((CHUNKS, 2)),
            sems((2,)),
            pltpu.SemaphoreType.REGULAR((2,)),
        ],
        compiler_params=pltpu.CompilerParams(
            collective_id=0, has_side_effects=True, vmem_limit_bytes=40 * 2**20
        ),
        cost_estimate=pl.CostEstimate(flops=2 * 10**8, bytes_accessed=2**20, transcendentals=10**6),
    )(*operands)


def solution(mesh):
    return jax.shard_map(
        per_device,
        mesh=mesh,
        in_specs=(
            P("seq", "tp"),
            P("seq", None, "tp"),
            P("seq", "tp"),
            P("seq", "tp"),
            P("seq"),
            P(None, "tp"),
            P(None, None, "tp"),
            P("tp"),
            P("tp"),
            P("tp"),
            P("tp"),
        ),
        out_specs=P("seq", "tp"),
        check_vma=False,
    )
```

time: 62.4 us -> 50.9 us (0.82)
  the two profiles are of different devices: /device:TPU:1 before, /device:TPU:385 now
where the time goes in v2:
time: 50.9 us; the launch traced here: 50.5 us
  Pallas kernels  44.2 us (87%)
  local copies, waits for them, and re-layouts  6.29 us (12%)
    pallas_call x1, Pallas kernels, per_device(): pl.pallas_call(functools.partial(kernel, nz, nx, ntp), out_shape=jax.Shap...  44.2 us
    unnamed x23, local copies, waits for them, and re-layouts  6.29 us

profile of v2, /device:TPU:385, one launch (start us, length us, event | category | flops | bytes accessed | tf_op | source)
XLA Modules:
  0.0 50.5 jit_solution(1362417083545790007)
XLA Ops:
  0.0 0.0 copy-start.4
  0.0 0.0 copy-start.10
  0.0 0.0 copy-start.7
  0.0 0.0 copy-start.8
  0.0 0.0 copy-start.9
  0.0 0.7 %copy-done.4 = f32[4,2,256]{2,1,0:T(2,128)S(1)} copy-done((f32[4,2,256]{2,1,0:T(2,128)S(1)}, f32[4,2,256]{2,1,0:T(2,128)}, u32[]{:S(2)}) %copy-start.4) | copy-done | bytes 8216
  0.7 0.0 copy-done.10
  0.7 0.0 copy-done.7
  0.7 0.0 copy-done.8
  0.7 0.0 copy-done.9
  0.7 0.0 copy-start
  0.7 0.9 %copy-done = bf16[128,1024]{1,0:T(8,128)(2,1)S(1)} copy-done((bf16[128,1024]{1,0:T(8,128)(2,1)S(1)}, bf16[128,1024]{1,0:T(8,128)(2,1)}, u32[]{:S(2)}) %copy-start) | copy-done | bytes 262168
  1.7 0.0 copy-start.1
  1.7 0.9 %copy-done.1 = bf16[128,1024]{1,0:T(8,128)(2,1)S(1)} copy-done((bf16[128,1024]{1,0:T(8,128)(2,1)S(1)}, bf16[128,1024]{1,0:T(8,128)(2,1)}, u32[]{:S(2)}) %copy-start.1) | copy-done | bytes 262168
  2.6 0.0 copy-start.2
  2.6 0.9 %copy-done.2 = bf16[128,2,256]{2,1,0:T(2,128)(2,1)S(1)} copy-done((bf16[128,2,256]{2,1,0:T(2,128)(2,1)S(1)}, bf16[128,2,256]{2,1,0:T(2,128)(2,1)}, u32[]{:S(2)}) %copy-start.2) | copy-done | bytes 131096
  3.5 0.0 copy-start.3
  3.5 0.7 %copy-done.3 = f32[4,1024]{1,0:T(4,128)S(1)} copy-done((f32[4,1024]{1,0:T(4,128)S(1)}, f32[4,1024]{1,0:T(4,128)}, u32[]{:S(2)}) %copy-start.3) | copy-done | bytes 16408
  4.2 0.0 copy-start.5
  4.2 0.7 %copy-done.5 = bf16[128,16]{0,1:T(8,128)(2,1)S(1)} copy-done((bf16[128,16]{0,1:T(8,128)(2,1)S(1)}, bf16[128,16]{0,1:T(8,128)(2,1)}, u32[]{:S(2)}) %copy-start.5) | copy-done | bytes 4120
  4.9 0.0 copy-start.6
  4.9 0.7 %copy-done.6 = f32[1024]{0:T(1024)S(1)} copy-done((f32[1024]{0:T(1024)S(1)}, f32[1024]{0:T(1024)}, u32[]{:S(2)}) %copy-start.6) | copy-done | bytes 4120
  5.6 44.2 %shard_map.109 = bf16[128,1024]{1,0:T(8,128)(2,1)S(1)} custom-call(bf16[128,1024]{1,0:T(8,128)(2,1)S(1)} %copy-done, bf16[128,2,256]{2,1,0:T(2,128)(2,1)S(1)} %copy-done.2, bf16[128,1024]{1,0:T(8,128)(2,1)S(1)} %copy-done.1, bf16[16,128]{1,0:T(8,128)(2,1)S(1)} %bitcast.6, s32[1,128]{1,0:T(1,128)S(1)} %bitcast.8, f32[4,1024]{1,0:T(4,128)S(1)} %copy-done.3, ...), custom_call_target="tpu_custom_call" | custom-call | flops 200000000 | bytes 1048576 | tf_op jit(solution)/shard_map/pallas_call | solution.py:448
  49.8 0.7 %copy.13 = bf16[128,1024]{1,0:T(8,128)(2,1)} copy(bf16[128,1024]{1,0:T(8,128)(2,1)S(1)} %shard_map.109) | data formatting | bytes 524288
Async XLA Ops:
  0.0 0.7 %copy-start.4 = (f32[4,2,256]{2,1,0:T(2,128)S(1)}, f32[4,2,256]{2,1,0:T(2,128)}, u32[]{:S(2)}) copy-start(f32[4,2,256]{2,1,0:T(2,128)} %cbc_hbm.1) | copy-start | bytes 24580
  0.0 0.7 %copy-start.10 = (f32[16]{0:T(128)S(1)}, f32[16]{0:T(128)}, u32[]{:S(2)}) copy-start(f32[16]{0:T(128)} %param.20) | copy-start | bytes 196
  0.0 0.7 %copy-start.7 = (s32[128]{0:T(128)S(1)}, s32[128]{0:T(128)}, u32[]{:S(2)}) copy-start(s32[128]{0:T(128)} %param.15) | copy-start | bytes 1540
  0.0 0.7 %copy-start.8 = (f32[16]{0:T(128)S(1)}, f32[16]{0:T(128)}, u32[]{:S(2)}) copy-start(f32[16]{0:T(128)} %param.18) | copy-start | bytes 196
  0.0 0.7 %copy-start.9 = (f32[16]{0:T(128)S(1)}, f32[16]{0:T(128)}, u32[]{:S(2)}) copy-start(f32[16]{0:T(128)} %param.19) | copy-start | bytes 196
  0.7 0.9 %copy-start = (bf16[128,1024]{1,0:T(8,128)(2,1)S(1)}, bf16[128,1024]{1,0:T(8,128)(2,1)}, u32[]{:S(2)}) copy-start(bf16[128,1024]{1,0:T(8,128)(2,1)} %x_hbm.1) | copy-start | bytes 786436
  1.7 0.9 %copy-start.1 = (bf16[128,1024]{1,0:T(8,128)(2,1)S(1)}, bf16[128,1024]{1,0:T(8,128)(2,1)}, u32[]{:S(2)}) copy-start(bf16[128,1024]{1,0:T(8,128)(2,1)} %z_hbm.1) | copy-start | bytes 786436
  2.6 0.9 %copy-start.2 = (bf16[128,2,256]{2,1,0:T(2,128)(2,1)S(1)}, bf16[128,2,256]{2,1,0:T(2,128)(2,1)}, u32[]{:S(2)}) copy-start(bf16[128,2,256]{2,1,0:T(2,128)(2,1)} %bc_hbm.1) | copy-start | bytes 393220
  3.5 0.7 %copy-start.3 = (f32[4,1024]{1,0:T(4,128)S(1)}, f32[4,1024]{1,0:T(4,128)}, u32[]{:S(2)}) copy-start(f32[4,1024]{1,0:T(4,128)} %cx_hbm.1) | copy-start | bytes 49156
  4.2 0.7 %copy-start.5 = (bf16[128,16]{0,1:T(8,128)(2,1)S(1)}, bf16[128,16]{0,1:T(8,128)(2,1)}, u32[]{:S(2)}) copy-start(bf16[128,16]{0,1:T(8,128)(2,1)} %param.14) | copy-start | bytes 12292
  4.9 0.7 %copy-start.6 = (f32[1024]{0:T(1024)S(1)}, f32[1024]{0:T(1024)}, u32[]{:S(2)}) copy-start(f32[1024]{0:T(1024)} %param.21) | copy-start | bytes 12292
